TPU v7x, 256 devices: a whole 4x4x8 slice. The times are simulated.
256 devices in a mesh: dp: 16 (over x, y), expert: 16 (over z, core).
Axes of the slice: x: 4, y: 4, z: 8, core: 2. Of those that a mesh axis runs over, the one named last changes fastest.
Arguments:
- tokens: bfloat16 [40960, 2048], P(('dp', 'expert')), may hold values from -6 to 6
- routes: int32 [40960, 2], P(('dp', 'expert')), may hold values from 0 to 15, all different within a row; in each aligned block of 160 rows (0 to 159, 160 to 319, ...) at most 30 rows name the same one
- route_gains: float32 [40960, 2], P(('dp', 'expert')), may hold values from 0.1 to 1
- cotangent: bfloat16 [40960, 2048], P(('dp', 'expert')), may hold values from -24 to 24
- w_gate: bfloat16 [16, 2048, 768], P('expert'), may hold values from -0.125 to 0.125
- w_up: bfloat16 [16, 2048, 768], P('expert'), may hold values from -0.125 to 0.125
- w_down: bfloat16 [16, 2048, 768], P('expert'), may hold values from -0.21875 to 0.21875
Outputs:
- layer_output: bfloat16 [40960, 2048], P(('dp', 'expert'))
- input_grad: bfloat16 [40960, 2048], P(('dp', 'expert'))
- grad_gate: bfloat16 [16, 2048, 768], P('expert', 'dp')
- grad_up: bfloat16 [16, 2048, 768], P('expert', 'dp')
- grad_down: bfloat16 [16, 2048, 768], P('expert', 'dp')
Inputs may be any that keep to these rules, and one draw needn't show every extreme that they name: `routes`: each row names 2 different experts. Within the rows of one device (aligned blocks of 160 rows) no expert is named more than 30 times, and in some device's rows one expert is named exactly 30 times.
All inputs are finite; a program needn't handle non-finite values.
Results may differ from a plain program's by a relative error of at most 0.015.
Values may be sent and summed in bfloat16 or wider, within the bound.
A program may use at most 128 MiB of HBM per device.

v0:
```python
import jax
import jax.numpy as jnp
from jax import lax
from jax.sharding import PartitionSpec as P

SLOTS = 32


def slot_masks(routes, experts):
    rows, picks = routes.shape
    chosen = routes.T.reshape(1, -1)
    labels = lax.broadcasted_iota(jnp.int32, (experts, rows * picks), 0)
    matches = chosen == labels
    total = rows * picks
    earlier = lax.broadcasted_iota(jnp.int32, (total, total), 0) < lax.broadcasted_iota(
        jnp.int32, (total, total), 1
    )
    before = jnp.dot(
        matches.astype(jnp.bfloat16),
        earlier.astype(jnp.bfloat16),
        preferred_element_type=jnp.float32,
    )
    position = jnp.sum(jnp.where(matches, before, 0.0), axis=0).astype(jnp.int32)
    target = chosen[0] * SLOTS + position
    slots = lax.broadcasted_iota(jnp.int32, (experts * SLOTS, total), 0)
    return (slots == target[None, :]).reshape(experts * SLOTS, picks, rows)


def rows_t(left, right):
    return lax.dot_general(
        left, right, (((1,), (1,)), ((), ())), preferred_element_type=jnp.float32
    )


def outer_rows(left, right):
    return lax.dot_general(
        left, right, (((0,), (0,)), ((), ())), preferred_element_type=jnp.float32
    )


def shards(tokens, routes, route_gains, cotangent, w_gate, w_up, w_down):
    experts = lax.axis_size("expert")
    groups = lax.axis_size("dp")
    width = tokens.shape[1]
    depth = width // groups
    flip = [(a * experts + b, b * experts + a) for a in range(groups) for b in range(experts)]
    mine = lax.axis_index("dp") * depth
    hidden_units = w_gate.shape[2]

    def fetch(w):
        part = lax.dynamic_slice_in_dim(w[0], mine, depth, axis=0)
        return part

    part = jnp.concatenate([fetch(w_gate), fetch(w_up), fetch(w_down)], axis=1)
    part = lax.ppermute(part, ("dp", "expert"), flip)
    full = lax.all_gather(part, "expert", axis=0, tiled=True)
    gate_mat = full[:, :hidden_units]
    up_mat = full[:, hidden_units : 2 * hidden_units]
    down_mat = full[:, 2 * hidden_units :]

    masks = slot_masks(routes, groups)
    first = masks[:, 0, :].astype(jnp.bfloat16)
    second = masks[:, 1, :].astype(jnp.bfloat16)
    both = first + second
    gains = route_gains.T
    slot_gain = jnp.sum(jnp.where(masks, gains[None], 0.0), axis=(1, 2))
    send_tok = jnp.dot(both, tokens, preferred_element_type=jnp.float32).astype(jnp.bfloat16)
    send_cot = (
        slot_gain[:, None] * jnp.dot(both, cotangent, preferred_element_type=jnp.float32)
    ).astype(jnp.bfloat16)

    def exchange(block):
        block = block.reshape(groups, SLOTS, width)
        block = lax.all_to_all(block, "dp", split_axis=0, concat_axis=0, tiled=True)
        return block.reshape(groups * SLOTS, width)

    arrived = exchange(send_tok)
    arrived_cot = exchange(send_cot)

    pre_gate = jnp.dot(arrived, gate_mat, preferred_element_type=jnp.float32)
    pre_up = jnp.dot(arrived, up_mat, preferred_element_type=jnp.float32)
    sigma = jax.nn.sigmoid(pre_gate)
    activated = pre_gate * sigma
    hidden = (activated * pre_up).astype(jnp.bfloat16)
    d_hidden = jnp.dot(arrived_cot, down_mat, preferred_element_type=jnp.float32)
    d_gate = (d_hidden * pre_up * (sigma * (1.0 + pre_gate * (1.0 - sigma)))).astype(jnp.bfloat16)
    d_up = (d_hidden * activated).astype(jnp.bfloat16)
    partial = jnp.concatenate(
        [outer_rows(arrived, d_gate), outer_rows(arrived, d_up), outer_rows(arrived_cot, hidden)],
        axis=1,
    ).astype(jnp.bfloat16)
    summed = lax.psum_scatter(partial, "expert", scatter_dimension=0, tiled=True)
    produced = rows_t(hidden, down_mat).astype(jnp.bfloat16)
    d_pick = (rows_t(d_gate, gate_mat) + rows_t(d_up, up_mat)).astype(jnp.bfloat16)
    back_out = exchange(produced)
    back_grad = exchange(d_pick)
    layer_output = (
        gains[0][:, None] * outer_rows(first, back_out)
        + gains[1][:, None] * outer_rows(second, back_out)
    ).astype(jnp.bfloat16)
    input_grad = (outer_rows(first, back_grad) + outer_rows(second, back_grad)).astype(
        jnp.bfloat16
    )
    summed = lax.ppermute(summed, ("dp", "expert"), flip)
    grad_gate = summed[None, :, :hidden_units]
    grad_up = summed[None, :, hidden_units : 2 * hidden_units]
    grad_down = summed[None, :, 2 * hidden_units :]
    return (layer_output, input_grad, grad_gate, grad_up, grad_down)


def solution(mesh):
    rows = P(("dp", "expert"), None)
    weights = P("expert", None, None)
    shares = P("expert", "dp", None)
    return jax.shard_map(
        shards,
        mesh=mesh,
        in_specs=(rows, rows, rows, rows, weights, weights, weights),
        out_specs=(rows, rows, shares, shares, shares),
        check_vma=False,
    )
```

profile of v0, /device:TPU:14, one launch (start us, length us, event | category | flops | bytes accessed | tf_op | source)
XLA Modules:
  0.0 330.9 jit_solution(815282746643636325)
XLA Ops:
  10.3 7.4 %collective-permute-start = (bf16[128,2304]{1,0:T(8,128)(2,1)S(1)}, bf16[128,2304]{1,0:T(8,128)(2,1)S(1)}, u32[]{:S(2)}, u32[]{:S(2)}) collective-permute-start(bf16[128,2304]{1,0:T(8,128)(2,1)S(1)} %pad_maximum_fusion.1), channel_id=1, source_target_pairs={{0,0},{1,16},{2,32},{3,48},{4,64},{5,80},{6,96},{7,112},{8,128},{9... | collective-permute-start | bytes 1769480 | tf_op jit(solution)/shard_map/ppermute | solution.py:55
  17.7 56.6 %collective-permute-done = bf16[128,2304]{1,0:T(8,128)(2,1)S(1)} collective-permute-done((bf16[128,2304]{1,0:T(8,128)(2,1)S(1)}, bf16[128,2304]{1,0:T(8,128)(2,1)S(1)}, u32[]{:S(2)}, u32[]{:S(2)}) %collective-permute-start) | collective-permute-done | bytes 589856 | tf_op jit(solution)/shard_map/ppermute | solution.py:55
  78.1 5.6 %all-to-all-start.2 = ((bf16[16,32,2048]{2,1,0:T(8,128)(2,1)}), bf16[16,32,2048]{2,1,0:T(8,128)(2,1)S(1)}, u32[]{:S(2)}, u32[]{:S(2)}) async-start(bf16[16,32,2048]{2,1,0:T(8,128)(2,1)} %bitcast.72), calls=%async_computation.2 | async-start | bytes 4194304 | tf_op jit(solution)/shard_map/all_to_all | solution.py:74
  85.8 23.9 %all-to-all-done.2 = bf16[16,32,2048]{2,1,0:T(8,128)(2,1)S(1)} async-done(((bf16[16,32,2048]{2,1,0:T(8,128)(2,1)}), bf16[16,32,2048]{2,1,0:T(8,128)(2,1)S(1)}, u32[]{:S(2)}, u32[]{:S(2)}) %all-to-all-start.2) | async-done | bytes 2097184 | tf_op jit(solution)/shard_map/all_to_all | solution.py:74
  109.6 7.3 %all-to-all-start = ((bf16[16,32,2048]{2,1,0:T(8,128)(2,1)}), bf16[16,32,2048]{2,1,0:T(8,128)(2,1)}, u32[]{:S(2)}, u32[]{:S(2)}) async-start(bf16[16,32,2048]{2,1,0:T(8,128)(2,1)} %bitcast.5), calls=%async_computation | async-start | bytes 4194304 | tf_op jit(solution)/shard_map/all_to_all | solution.py:74
  117.2 18.1 %all-gather.2.cloned.1.call-done = bf16[2048,2304]{1,0:T(8,128)(2,1)} async-done(((bf16[128,2304]{1,0:T(8,128)(2,1)}), bf16[2048,2304]{1,0:T(8,128)(2,1)}) %all-gather.2.cloned.1.call-update) | async-done | bytes 9437200 | tf_op jit(solution)/shard_map/all_gather | solution.py:56
  135.3 4.8 %fusion = f32[512,768]{1,0:T(8,128)} fusion(bf16[512,2048]{1,0:T(8,128)(2,1)S(1)} %bitcast.68, bf16[2048,2304]{1,0:T(8,128)(2,1)} %all-gather.2.cloned.1.call-done), kind=kOutput, calls=%fused_computation.8 | convolution fusion | flops 1610612736 | bytes 6815744 | tf_op jit(solution)/shard_map/dot_general | solution.py:85
  140.2 4.4 %fusion.5 = f32[512,768]{1,0:T(8,128)S(1)} fusion(bf16[512,2048]{1,0:T(8,128)(2,1)} %bitcast.6, bf16[2048,2304]{1,0:T(8,128)(2,1)} %all-gather.2.cloned.1.call-done), kind=kOutput, calls=%fused_computation.13 | convolution fusion | flops 1610612736 | bytes 6815744 | tf_op jit(solution)/shard_map/dot_general | solution.py:81
  144.7 5.0 %multiply_convert_fusion.2 = (bf16[512,768]{1,0:T(8,128)(2,1)S(1)}, bf16[512,768]{1,0:T(8,128)(2,1)S(1)}, bf16[512,768]{1,0:T(8,128)(2,1)S(1)}) fusion(f32[512,768]{1,0:T(8,128)S(1)} %copy-done.16, f32[512,768]{1,0:T(8,128)S(1)} %fusion.5, bf16[512,2048]{1,0:T(8,128)(2,1)} %bitcast.6, bf16[2048,2304]{1,0:T(8,128)(2,1)} %all-gather.2.cloned.1.call-done), kind=kOutput, calls=%fused_computation.25 | convolution fusion | flops 1616510976 | bytes 10747904 | tf_op jit(solution)/shard_map/dot_general | solution.py:80
  151.6 3.4 %convolution_convert_fusion.1 = bf16[2048,768]{0,1:T(8,128)(2,1)S(1)} fusion(bf16[512,2048]{1,0:T(8,128)(2,1)} %bitcast.6, bf16[512,768]{1,0:T(8,128)(2,1)S(1)} %get-tuple-element.26), kind=kOutput, calls=%fused_computation.4 | convolution fusion | flops 1612185600 | bytes 6029312 | tf_op jit(solution)/shard_map/dot_general | solution.py:36
  155.0 3.4 %convolution_convert_fusion.2 = bf16[2048,768]{0,1:T(8,128)(2,1)S(1)} fusion(bf16[512,2048]{1,0:T(8,128)(2,1)} %bitcast.6, bf16[512,768]{1,0:T(8,128)(2,1)S(1)} %get-tuple-element.25), kind=kOutput, calls=%fused_computation.5 | convolution fusion | flops 1612185600 | bytes 6029312 | tf_op jit(solution)/shard_map/dot_general | solution.py:36
  158.5 4.7 %pad_maximum_fusion = bf16[2048,2304]{0,1:T(8,128)(2,1)} fusion(bf16[2048,768]{0,1:T(8,128)(2,1)S(1)} %convolution_convert_fusion, bf16[2048,768]{0,1:T(8,128)(2,1)S(1)} %convolution_convert_fusion.1, bf16[2048,768]{0,1:T(8,128)(2,1)S(1)} %convolution_convert_fusion.2), kind=kLoop, calls=%fused_computation | loop fusion | flops 28311552 | bytes 18874368 | tf_op jit(solution)/shard_map/concatenate | solution.py:88
  163.1 12.4 %copy.25 = bf16[2048,2304]{1,0:T(8,128)(2,1)} copy(bf16[2048,2304]{0,1:T(8,128)(2,1)} %pad_maximum_fusion) | data formatting | bytes 18874368
  176.6 3.8 %fusion.3 = f32[512,2048]{1,0:T(8,128)S(1)} fusion(bf16[512,768]{1,0:T(8,128)(2,1)S(1)} %copy-done.15, bf16[2048,2304]{1,0:T(8,128)(2,1)} %all-gather.2.cloned.1.call-done), kind=kOutput, calls=%fused_computation.11 | convolution fusion | flops 1610612736 | bytes 8126464 | tf_op jit(solution)/shard_map/dot_general | solution.py:30
  180.4 5.1 %add_convert_fusion = bf16[512,2048]{1,0:T(8,128)(2,1)} fusion(f32[512,2048]{1,0:T(8,128)S(1)} %fusion.3, bf16[512,768]{1,0:T(8,128)(2,1)S(1)} %copy-done.13, bf16[2048,2304]{1,0:T(8,128)(2,1)} %all-gather.2.cloned.1.call-done), kind=kOutput, calls=%fused_computation.1 | convolution fusion | flops 1612709888 | bytes 10223616 | tf_op jit(solution)/shard_map/dot_general | solution.py:30
  185.5 8.2 %all-to-all-start.3 = ((bf16[16,32,2048]{2,1,0:T(8,128)(2,1)}), bf16[16,32,2048]{2,1,0:T(8,128)(2,1)S(1)}, u32[]{:S(2)}, u32[]{:S(2)}) async-start(bf16[16,32,2048]{2,1,0:T(8,128)(2,1)} %bitcast.71), calls=%async_computation.3 | async-start | bytes 4194304 | tf_op jit(solution)/shard_map/all_to_all | solution.py:74
  193.8 5.0 %convolution_convert_fusion.4 = bf16[512,2048]{1,0:T(8,128)(2,1)} fusion(bf16[512,768]{1,0:T(8,128)(2,1)S(1)} %copy-done.18, bf16[2048,2304]{1,0:T(8,128)(2,1)} %all-gather.2.cloned.1.call-done), kind=kOutput, calls=%fused_computation.7 | convolution fusion | flops 1611661312 | bytes 6029312 | tf_op jit(solution)/shard_map/dot_general | solution.py:30
  198.8 21.2 %all-to-all-done.3 = bf16[16,32,2048]{2,1,0:T(8,128)(2,1)S(1)} async-done(((bf16[16,32,2048]{2,1,0:T(8,128)(2,1)}), bf16[16,32,2048]{2,1,0:T(8,128)(2,1)S(1)}, u32[]{:S(2)}, u32[]{:S(2)}) %all-to-all-start.3) | async-done | bytes 2097184 | tf_op jit(solution)/shard_map/all_to_all | solution.py:74
  221.3 7.0 %all-to-all-start.1 = ((bf16[16,32,2048]{2,1,0:T(8,128)(2,1)}), bf16[16,32,2048]{2,1,0:T(8,128)(2,1)S(1)}, u32[]{:S(2)}, u32[]{:S(2)}) async-start(bf16[16,32,2048]{2,1,0:T(8,128)(2,1)} %bitcast.70), calls=%async_computation.1 | async-start | bytes 4194304 | tf_op jit(solution)/shard_map/all_to_all | solution.py:74
  228.4 2.3 fusion.15
  232.1 20.1 %reduce-scatter.4.cloned.1.call-done = bf16[128,2304]{1,0:T(8,128)(2,1)} async-done(((bf16[2048,2304]{1,0:T(8,128)(2,1)}), bf16[128,2304]{1,0:T(8,128)(2,1)}) %reduce-scatter.4.cloned.1.call-update) | async-done | bytes 589840
  252.2 2.1 copy.26
  258.2 3.2 fusion.12
  261.3 57.5 %collective-permute-done.1 = bf16[128,2304]{0,1:T(8,128)(2,1)} collective-permute-done((bf16[128,2304]{0,1:T(8,128)(2,1)}, bf16[128,2304]{0,1:T(8,128)(2,1)}, u32[]{:S(2)}, u32[]{:S(2)}) %collective-permute-start.1) | collective-permute-done | bytes 589856 | tf_op jit(solution)/shard_map/ppermute | solution.py:104
  (67 shorter events, 23.9 us)
Async XLA Ops:
  7.2 1.9 copy-start
  7.2 68.0 %copy-start.10 = (f32[160,2]{0,1:T(2,128)S(1)}, f32[160,2]{0,1:T(2,128)}, u32[]{:S(2)}) copy-start(f32[160,2]{0,1:T(2,128)} %param.9) | copy-start | bytes 3844
  7.2 68.1 %copy-start.9 = (s32[160,2]{0,1:T(2,128)S(1)}, s32[160,2]{0,1:T(2,128)}, u32[]{:S(2)}) copy-start(s32[160,2]{0,1:T(2,128)} %param.8) | copy-start | bytes 3844
  7.2 128.1 %all-gather.2.cloned.1.call-start = ((), (), s32[]{:S(2)}) async-start(), calls=%async_computation.5 | async-start | bytes 10027008 | tf_op jit(solution)/shard_map/all_gather | solution.py:56
  9.1 66.9 %copy-start.11 = (bf16[160,2048]{1,0:T(8,128)(2,1)S(1)}, bf16[160,2048]{1,0:T(8,128)(2,1)}, u32[]{:S(2)}) copy-start(bf16[160,2048]{1,0:T(8,128)(2,1)} %param.10) | copy-start | bytes 1966084
  10.3 64.1 %collective-permute-start = (bf16[128,2304]{1,0:T(8,128)(2,1)S(1)}, bf16[128,2304]{1,0:T(8,128)(2,1)S(1)}, u32[]{:S(2)}, u32[]{:S(2)}) collective-permute-start(bf16[128,2304]{1,0:T(8,128)(2,1)S(1)} %pad_maximum_fusion.1), channel_id=1, source_target_pairs={{0,0},{1,16},{2,32},{3,48},{4,64},{5,80},{6,96},{7,112},{8,128},{9... | collective-permute-start | bytes 1769480 | tf_op jit(solution)/shard_map/ppermute | solution.py:55
  78.1 5.6 %copy-start.7 = (bf16[160,2048]{1,0:T(8,128)(2,1)S(1)}, bf16[160,2048]{1,0:T(8,128)(2,1)}, u32[]{:S(2)}) copy-start(bf16[160,2048]{1,0:T(8,128)(2,1)} %param.7) | copy-start | bytes 1966084
  78.1 31.5 %all-to-all-start.2 = ((bf16[16,32,2048]{2,1,0:T(8,128)(2,1)}), bf16[16,32,2048]{2,1,0:T(8,128)(2,1)S(1)}, u32[]{:S(2)}, u32[]{:S(2)}) async-start(bf16[16,32,2048]{2,1,0:T(8,128)(2,1)} %bitcast.72), calls=%async_computation.2 | async-start | bytes 4194304 | tf_op jit(solution)/shard_map/all_to_all | solution.py:74
  109.6 25.7 %copy-start.5 = (bf16[16,32,2048]{2,1,0:T(8,128)(2,1)}, bf16[16,32,2048]{2,1,0:T(8,128)(2,1)S(1)}, u32[]{:S(2)}) copy-start(bf16[16,32,2048]{2,1,0:T(8,128)(2,1)S(1)} %all-to-all-done.2) | copy-start | bytes 6291460
  109.6 30.6 %all-to-all-start = ((bf16[16,32,2048]{2,1,0:T(8,128)(2,1)}), bf16[16,32,2048]{2,1,0:T(8,128)(2,1)}, u32[]{:S(2)}, u32[]{:S(2)}) async-start(bf16[16,32,2048]{2,1,0:T(8,128)(2,1)} %bitcast.5), calls=%async_computation | async-start | bytes 4194304 | tf_op jit(solution)/shard_map/all_to_all | solution.py:74
  117.0 135.2 %reduce-scatter.4.cloned.1.call-start = ((), (), s32[]{:S(2)}) async-start(), calls=%async_computation.6 | async-start | bytes 10027008
  140.2 4.4 %copy-start.16 = (f32[512,768]{1,0:T(8,128)S(1)}, f32[512,768]{1,0:T(8,128)}, u32[]{:S(2)}) copy-start(f32[512,768]{1,0:T(8,128)} %fusion) | copy-start | bytes 4718596
  144.7 5.0 %copy-start.6 = (bf16[16,32,2048]{2,1,0:T(8,128)(2,1)S(1)}, bf16[16,32,2048]{2,1,0:T(8,128)(2,1)}, u32[]{:S(2)}) copy-start(bf16[16,32,2048]{2,1,0:T(8,128)(2,1)} %copy-done.5) | copy-start | bytes 6291460
  149.7 1.9 copy-start.17
  149.7 1.9 copy-start.14
  149.7 5.3 %copy-start.12 = (bf16[512,768]{1,0:T(8,128)(2,1)}, bf16[512,768]{1,0:T(8,128)(2,1)S(1)}, u32[]{:S(2)}) copy-start(bf16[512,768]{1,0:T(8,128)(2,1)S(1)} %get-tuple-element.25) | copy-start | bytes 2359300
  176.6 3.8 %copy-start.13 = (bf16[512,768]{1,0:T(8,128)(2,1)S(1)}, bf16[512,768]{1,0:T(8,128)(2,1)}, u32[]{:S(2)}) copy-start(bf16[512,768]{1,0:T(8,128)(2,1)} %copy-done.12) | copy-start | bytes 2359300
  185.5 8.3 %copy-start.18 = (bf16[512,768]{1,0:T(8,128)(2,1)S(1)}, bf16[512,768]{1,0:T(8,128)(2,1)}, u32[]{:S(2)}) copy-start(bf16[512,768]{1,0:T(8,128)(2,1)} %copy-done.17) | copy-start | bytes 2359300
  185.5 34.5 %all-to-all-start.3 = ((bf16[16,32,2048]{2,1,0:T(8,128)(2,1)}), bf16[16,32,2048]{2,1,0:T(8,128)(2,1)S(1)}, u32[]{:S(2)}, u32[]{:S(2)}) async-start(bf16[16,32,2048]{2,1,0:T(8,128)(2,1)} %bitcast.71), calls=%async_computation.3 | async-start | bytes 4194304 | tf_op jit(solution)/shard_map/all_to_all | solution.py:74
  221.3 34.9 %all-to-all-start.1 = ((bf16[16,32,2048]{2,1,0:T(8,128)(2,1)}), bf16[16,32,2048]{2,1,0:T(8,128)(2,1)S(1)}, u32[]{:S(2)}, u32[]{:S(2)}) async-start(bf16[16,32,2048]{2,1,0:T(8,128)(2,1)} %bitcast.70), calls=%async_computation.1 | async-start | bytes 4194304 | tf_op jit(solution)/shard_map/all_to_all | solution.py:74
  228.4 2.4 copy-start.4
  254.4 64.5 %collective-permute-start.1 = (bf16[128,2304]{0,1:T(8,128)(2,1)}, bf16[128,2304]{0,1:T(8,128)(2,1)}, u32[]{:S(2)}, u32[]{:S(2)}) collective-permute-start(bf16[128,2304]{0,1:T(8,128)(2,1)} %copy.26), channel_id=1, source_target_pairs={{0,0},{1,16},{2,32},{3,48},{4,64},{5,80},{6,96},{7,112},{8,128},{9... | collective-permute-start | bytes 1769480 | tf_op jit(solution)/shard_map/ppermute | solution.py:104
  256.3 1.4 copy-start.2
  258.2 65.9 %copy-start.1 = (bf16[1,2048,768]{2,1,0:T(8,128)(2,1)S(1)}, bf16[1,2048,768]{2,1,0:T(8,128)(2,1)}, u32[]{:S(2)}) copy-start(bf16[1,2048,768]{2,1,0:T(8,128)(2,1)} %param.11) | copy-start | bytes 9437188
  (3 other events, 3.3 us)
Sparse Core Ops, SparseCore 0:
  75.3 59.9 all-gather.1
  175.6 76.5 reduce-scatter.3
where the time goes:
time: 332 us; the launch traced here: 331 us
  waiting for transfers between devices  198 us (60%)
  matrix products  48.6 us (15%)
  starting transfers between devices  37.8 us (11%)
  local copies, waits for them, and re-layouts  27.6 us (8%)
  between operations  14.3 us (4%)
  other arithmetic  5.04 us (2%)
    ppermute x1, waiting for transfers between devices, shards(): summed = lax.ppermute(summed, ('dp', 'expert'), flip)  57.5 us
    ppermute x1, waiting for transfers between devices, shards(): part = lax.ppermute(part, ('dp', 'expert'), flip)  56.6 us
    all_to_all x4, waiting for transfers between devices, exchange(): block = lax.all_to_all(block, 'dp', split_axis=0, concat_axis=0, tiled=True)  45.1 us
    all_to_all x4, starting transfers between devices, exchange(): block = lax.all_to_all(block, 'dp', split_axis=0, concat_axis=0, tiled=True)  28.2 us
    unnamed x43, local copies, waits for them, and re-layouts  24.4 us
    unnamed x3, waiting for transfers between devices  20.2 us
    all_gather x1, waiting for transfers between devices, shards(): full = lax.all_gather(part, 'expert', axis=0, tiled=True)  18.1 us
    dot_general x7, matrix products, outer_rows(): lax.dot_general(left, right, (((0,), (0,)), ((), ())), preferred_element_...  16.1 us
  transfers between devices with their start and end apart: 8, of which 7 were waited for; matrix products, arithmetic and copies ran while one was open for 10% of the time, Pallas kernels for 0%

commit v1 on v0

v1 whole, which is shorter than its diff:
```python
import functools

import jax
import jax.numpy as jnp
from jax import lax
from jax.experimental import pallas as pl
from jax.experimental.pallas import tpu as pltpu
from jax.sharding import PartitionSpec as P

SLOTS = 32
LANES = 128
CHUNK = 256
QUARTERS = 4
MESH = pl.DeviceIdType.MESH
F32 = jnp.float32
BF16 = jnp.bfloat16


def slot_masks(routes, experts):
    rows, picks = routes.shape
    total = rows * picks
    chosen = routes.T.reshape(1, -1)
    labels = lax.broadcasted_iota(jnp.int32, (experts, total), 0)
    matches = chosen == labels
    earlier = lax.broadcasted_iota(jnp.int32, (total, total), 0) < lax.broadcasted_iota(
        jnp.int32, (total, total), 1
    )
    before = jnp.dot(matches.astype(BF16), earlier.astype(BF16), preferred_element_type=F32)
    position = jnp.sum(jnp.where(matches, before, 0.0), axis=0).astype(jnp.int32)
    target = (chosen[0] * SLOTS + position).reshape(picks, rows)
    slots = lax.broadcasted_iota(jnp.int32, (picks, experts * SLOTS, rows), 1)
    return slots == target[:, None, :], target


def dot(a, b):
    return jnp.dot(a, b, preferred_element_type=F32)


def dot_rows(a, b):
    return lax.dot_general(a, b, (((1,), (1,)), ((), ())), preferred_element_type=F32)


def dot_outer(a, b):
    return lax.dot_general(a, b, (((0,), (0,)), ((), ())), preferred_element_type=F32)


def moe_kernel(
    n,
    nz,
    both_ref,
    first_ref,
    second_ref,
    slot_gain_ref,
    gains_ref,
    tok_ref,
    cot_ref,
    wg_ref,
    wu_ref,
    wd_ref,
    out_ref,
    ingrad_ref,
    gg_ref,
    gu_ref,
    gd_ref,
    w_buf,
    st,
    sc,
    x_buf,
    c_buf,
    hid,
    dgate,
    dup,
    dpart,
    dx_buf,
    ch_buf,
    po,
    pg,
    bo,
    bg,
    fg,
    loc_sem,
    w_recv,
    x_recv,
    ch_recv,
    dx_recv,
    one_sem,
):
    (TS, TR, TL, CS, CR, CL, OS, OR, OL, GS, GR, GL, WS, PS, XS, HS, DS, FS, FR, FL) = range(20)
    width = tok_ref.shape[1]
    chunks = w_buf.shape[1]
    rows = n * SLOTS
    quarter = width // QUARTERS
    depth = width // n
    block = 256
    row_block = min(block, rows)

    d = lax.axis_index("dp")
    ex = lax.axis_index("expert")
    z = lax.div(ex, 2)
    c = lax.rem(ex, 2)
    sgn = 1 - 2 * c
    r = lax.rem(sgn * (z - lax.div(d, 2)) + nz, nz)
    nxt = 2 * lax.rem(z + sgn + nz, nz) + c
    prv = 2 * lax.rem(z - sgn + nz, nz) + c
    mate = ex + sgn
    native = ex == d
    rootmate = mate == d

    def remote(src, dst, send, recv, dev):
        return pltpu.make_async_remote_copy(
            src_ref=src, dst_ref=dst, send_sem=send, recv_sem=recv, device_id=dev, device_id_type=MESH
        )

    def wait_bytes(ref, sem):
        pltpu.make_async_copy(ref, ref, sem).wait()

    barrier = pltpu.get_barrier_semaphore()

    def greet(dev):
        pl.semaphore_signal(barrier, inc=1, device_id=dev, device_id_type=MESH)

    @pl.loop(1, n)
    def _(j):
        greet((lax.rem(d + j, n), ex))

    greet((d, mate))
    greet((d, nxt))
    greet((d, prv))

    @pl.when(d != ex)
    def _():
        greet((ex, mate))

    @pl.when(rootmate)
    def _():
        @pl.loop(1, n)
        def _(j):
            greet((lax.rem(d + j, n), d))

    @pl.when(native)
    def _():
        for k in range(chunks):
            for m, ref in enumerate((wg_ref, wu_ref, wd_ref)):
                for h in range(2):
                    pltpu.make_async_copy(
                        ref.at[0, :, pl.ds(CHUNK * k + LANES * h, LANES)],
                        w_buf.at[h, k, m],
                        loc_sem.at[3 * k + m],
                    ).start()

    pl.semaphore_wait(
        barrier, n + 2 + jnp.where(d != ex, 1, 0) + jnp.where(rootmate, n - 1, 0)
    )

    def slot_rows(i):
        return pl.ds(pl.multiple_of(i * SLOTS, SLOTS), SLOTS)

    def exchange(src, dst, send, recv, own):
        pltpu.make_async_copy(src.at[slot_rows(d)], dst.at[slot_rows(d)], one_sem.at[own]).start()

        @pl.loop(1, n)
        def _(j):
            t = lax.rem(d + j, n)
            remote(
                src.at[slot_rows(t)], dst.at[slot_rows(d)], one_sem.at[send], one_sem.at[recv], (t, ex)
            ).start()

    def exchanged(dst, recv, own):
        wait_bytes(dst.at[pl.ds(0, SLOTS)], one_sem.at[own])
        wait_bytes(dst.at[pl.ds(0, rows - SLOTS)], one_sem.at[recv])

    def cols(i, size=block):
        return pl.ds(pl.multiple_of(i * size, size), size)

    def piece(buf, k, m, q):
        return buf.at[k, m, pl.ds(pl.multiple_of(q * quarter, quarter), quarter)]

    def weights(k):
        @pl.loop(0, 3)
        def _(m):
            km = 3 * k + m

            @pl.when(native)
            def _():
                wait_bytes(w_buf.at[:, k, m], loc_sem.at[km])

            @pl.loop(0, QUARTERS)
            def _(q):
                i = QUARTERS * km + q
                mine = piece(w_buf.at[c], k, m, q)

                @pl.when(jnp.logical_not(native))
                def _():
                    wait_bytes(mine, w_recv.at[i])

                @pl.when(r <= nz - 2)
                def _():
                    remote(mine, mine, one_sem.at[WS], w_recv.at[i], (d, nxt)).start()

                @pl.when(native)
                def _():
                    other = piece(w_buf.at[1 - c], k, m, q)
                    remote(other, other, one_sem.at[PS], w_recv.at[i], (d, mate)).start()

            @pl.when(jnp.logical_not(rootmate))
            def _():
                half = w_buf.at[c, k, m]
                remote(half, half, one_sem.at[XS], x_recv.at[km], (d, mate)).start()

    def swapped(k):
        @pl.when(jnp.logical_not(native))
        def _():
            @pl.loop(0, 3)
            def _(m):
                wait_bytes(w_buf.at[1 - c, k, m], x_recv.at[3 * k + m])

    def mat(k, m):
        return jnp.concatenate([w_buf[0, k, m], w_buf[1, k, m]], axis=1)

    def hidden_units(k):
        @pl.loop(0, rows // row_block)
        def _(i):
            sl = cols(i, row_block)
            x = x_buf[sl, :]
            gate = dot(x, mat(k, 0))
            up = dot(x, mat(k, 1))
            sigma = jax.nn.sigmoid(gate)
            act = gate * sigma
            hid[k, sl, :] = (act * up).astype(BF16)
            dh = dot(c_buf[sl, :], mat(k, 2))
            dgate[k, sl, :] = (dh * up * (sigma * (1.0 + gate * (1.0 - sigma)))).astype(BF16)
            dup[k, sl, :] = (dh * act).astype(BF16)

    def outer(k):
        @pl.loop(0, width // block)
        def _(i):
            sl = cols(i)
            pair = jnp.concatenate([dgate[k], dup[k]], axis=1)
            both = dot_outer(x_buf[:, sl], pair).astype(BF16)
            down = dot_outer(c_buf[:, sl], hid[k]).astype(BF16)
            dpart[0, k, 0, sl, :] = both[:, :LANES]
            dpart[1, k, 0, sl, :] = both[:, LANES:CHUNK]
            dpart[0, k, 1, sl, :] = both[:, CHUNK : CHUNK + LANES]
            dpart[1, k, 1, sl, :] = both[:, CHUNK + LANES :]
            dpart[0, k, 2, sl, :] = down[:, :LANES]
            dpart[1, k, 2, sl, :] = down[:, LANES:]

        remote(dpart.at[1 - c, k], dx_buf.at[k], one_sem.at[DS], dx_recv.at[k], (d, mate)).start()

    def rows_of(k, m, sl):
        return jnp.concatenate([w_buf[0, k, m, sl, :], w_buf[1, k, m, sl, :]], axis=1)

    def produce():
        @pl.loop(0, width // block)
        def _(i):
            sl = cols(i)
            acc = dot_rows(hid[0], rows_of(0, 2, sl))
            for k in range(1, chunks):
                acc += dot_rows(hid[k], rows_of(k, 2, sl))
            po[:, sl] = acc.astype(BF16)

    def pick_grads():
        @pl.loop(0, width // block)
        def _(i):
            sl = cols(i)
            acc = dot_rows(dgate[0], rows_of(0, 0, sl))
            acc += dot_rows(dup[0], rows_of(0, 1, sl))
            for k in range(1, chunks):
                acc += dot_rows(dgate[k], rows_of(k, 0, sl))
                acc += dot_rows(dup[k], rows_of(k, 1, sl))
            pg[:, sl] = acc.astype(BF16)

    def chain(k):
        wait_bytes(dx_buf.at[k], dx_recv.at[k])

        @pl.loop(0, 3)
        def _(m):
            km = 3 * k + m

            @pl.loop(0, QUARTERS)
            def _(q):
                i = QUARTERS * km + q
                sl = pl.ds(pl.multiple_of(q * quarter, quarter), quarter)
                mine = piece(dpart.at[c], k, m, q)
                there = piece(ch_buf, k, m, q)
                own = dpart[c, k, m, sl, :].astype(F32) + dx_buf[k, m, sl, :].astype(F32)

                @pl.when(r == 1)
                def _():
                    dpart[c, k, m, sl, :] = own.astype(BF16)

                @pl.when(r != 1)
                def _():
                    wait_bytes(there, ch_recv.at[i])
                    dpart[c, k, m, sl, :] = (own + ch_buf[k, m, sl, :].astype(F32)).astype(BF16)

                @pl.when(r != 0)
                def _():
                    remote(mine, there, one_sem.at[HS], ch_recv.at[i], (d, nxt)).start()

            @pl.when(r == 0)
            def _():
                def share(t):
                    return dpart.at[c, k, m, pl.ds(pl.multiple_of(t * depth, depth), depth)]

                @pl.when(native)
                def _():
                    pltpu.make_async_copy(share(d), fg.at[c, k, m], one_sem.at[FL]).start()

                @pl.when(rootmate)
                def _():
                    remote(
                        share(d), fg.at[c, k, m], one_sem.at[FS], one_sem.at[FR], (d, d)
                    ).start()

                @pl.loop(1, n)
                def _(j):
                    t = lax.rem(d + j, n)
                    remote(
                        share(t), fg.at[c, k, m], one_sem.at[FS], one_sem.at[FR], (t, d)
                    ).start()

    @pl.loop(0, width // 512)
    def _(i):
        sl = cols(i, 512)
        st[:, sl] = dot(both_ref[...], tok_ref[:, sl]).astype(BF16)

    exchange(st, x_buf, TS, TR, TL)

    @pl.loop(0, width // 512)
    def _(i):
        sl = cols(i, 512)
        sc[:, sl] = (slot_gain_ref[...] * dot(both_ref[...], cot_ref[:, sl])).astype(BF16)

    exchange(sc, c_buf, CS, CR, CL)

    @pl.loop(0, chunks)
    def _(k):
        weights(k)

    exchanged(x_buf, TR, TL)
    exchanged(c_buf, CR, CL)

    @pl.loop(0, chunks)
    def _(k):
        swapped(k)
        hidden_units(k)
        outer(k)

    produce()
    exchange(po, bo, OS, OR, OL)
    pick_grads()
    exchange(pg, bg, GS, GR, GL)

    @pl.loop(0, chunks)
    def _(k):
        chain(k)

    exchanged(bo, OR, OL)
    gain = gains_ref[...]

    @pl.loop(0, width // 512)
    def _(i):
        sl = cols(i, 512)
        got = bo[:, sl]
        out_ref[:, sl] = (
            gain[:, 0:1] * dot(first_ref[...], got) + gain[:, 1:2] * dot(second_ref[...], got)
        ).astype(BF16)

    exchanged(bg, GR, GL)

    @pl.loop(0, width // 512)
    def _(i):
        sl = cols(i, 512)
        got = bg[:, sl]
        ingrad_ref[:, sl] = (dot(first_ref[...], got) + dot(second_ref[...], got)).astype(BF16)

    @pl.when(native)
    def _():
        wait_bytes(fg.at[0], one_sem.at[FL])
        wait_bytes(fg.at[0], one_sem.at[FR])
        wait_bytes(dpart.at[0, :, :, pl.ds(0, width - depth)], one_sem.at[FS])

    @pl.when(jnp.logical_not(native))
    def _():
        wait_bytes(fg, one_sem.at[FR])

    @pl.when(rootmate)
    def _():
        wait_bytes(dpart.at[0], one_sem.at[FS])

    for k in range(chunks):
        for h in range(2):
            sl = slice(CHUNK * k + LANES * h, CHUNK * k + LANES * (h + 1))
            gg_ref[0, :, sl] = fg[h, k, 0]
            gu_ref[0, :, sl] = fg[h, k, 1]
            gd_ref[0, :, sl] = fg[h, k, 2]

    for send, buf in ((TS, st), (CS, sc), (OS, po), (GS, pg)):
        wait_bytes(buf.at[pl.ds(0, rows - SLOTS)], one_sem.at[send])

    @pl.when(r <= nz - 2)
    def _():
        wait_bytes(w_buf.at[0], one_sem.at[WS])

    @pl.when(native)
    def _():
        wait_bytes(w_buf.at[0], one_sem.at[PS])

    @pl.when(jnp.logical_not(rootmate))
    def _():
        wait_bytes(w_buf.at[0], one_sem.at[XS])

    @pl.when(r != 0)
    def _():
        wait_bytes(ch_buf, one_sem.at[HS])

    wait_bytes(dx_buf, one_sem.at[DS])


def shards(n, tokens, routes, route_gains, cotangent, w_gate, w_up, w_down):
    width = tokens.shape[1]
    units = w_gate.shape[2]
    chunks = units // CHUNK
    count = tokens.shape[0]
    depth = width // n
    rows = n * SLOTS

    masks, target = slot_masks(routes, n)
    both = (masks[0] | masks[1]).astype(BF16)
    gains = route_gains.T
    slot_gain = jnp.sum(jnp.where(masks, gains[:, None, :], 0.0), axis=(0, 2))[:, None]
    slots = lax.broadcasted_iota(jnp.int32, (count, rows), 1)
    first = (slots == target[0][:, None]).astype(BF16)
    second = (slots == target[1][:, None]).astype(BF16)

    vmem = pl.BlockSpec(memory_space=pltpu.VMEM)
    anywhere = pl.BlockSpec(memory_space=pl.ANY)
    sem = pltpu.SemaphoreType.DMA
    share = jax.ShapeDtypeStruct((1, depth, units), BF16)
    row_out = jax.ShapeDtypeStruct((count, width), BF16)
    landed = pltpu.VMEM((rows, width), BF16)
    acts = pltpu.VMEM((chunks, rows, CHUNK), BF16)
    half = pltpu.VMEM((chunks, 3, width, LANES), BF16)
    halves = pltpu.VMEM((2, chunks, 3, width, LANES), BF16)
    return pl.pallas_call(
        functools.partial(moe_kernel, n, n // 2),
        out_shape=(row_out, row_out, share, share, share),
        in_specs=[vmem] * 7 + [anywhere] * 3,
        out_specs=(vmem,) * 5,
        scratch_shapes=[
            halves,
            landed,
            landed,
            landed,
            landed,
            acts,
            acts,
            acts,
            halves,
            half,
            half,
            landed,
            landed,
            landed,
            landed,
            pltpu.VMEM((2, chunks, 3, depth, LANES), BF16),
            sem((3 * chunks,)),
            sem((3 * chunks * QUARTERS,)),
            sem((3 * chunks,)),
            sem((3 * chunks * QUARTERS,)),
            sem((chunks,)),
            sem((20,)),
        ],
        compiler_params=pltpu.CompilerParams(
            collective_id=0, has_side_effects=True, vmem_limit_bytes=60 * 2**20
        ),
    )(both, first, second, slot_gain, route_gains, tokens, cotangent, w_gate, w_up, w_down)


def solution(mesh):
    rows = P(("dp", "expert"), None)
    weights = P("expert", None, None)
    shares = P("expert", "dp", None)
    return jax.shard_map(
        functools.partial(shards, mesh.shape["dp"]),
        mesh=mesh,
        in_specs=(rows, rows, rows, rows, weights, weights, weights),
        out_specs=(rows, rows, shares, shares, shares),
        check_vma=False,
    )
```

time: 332 us -> 227 us (0.68)
  the two profiles are of different devices: /device:TPU:14 before, /device:TPU:161 now
where the time goes in v1:
time: 227 us; the launch traced here: 226 us
  Pallas kernels  212 us (93%)
  local copies, waits for them, and re-layouts  10.2 us (4%)
  other arithmetic  3.36 us (1%)
    pallas_call x1, Pallas kernels, shards(): pl.pallas_call(functools.partial(moe_kernel, n, n // 2), out_shape=(row_o...  212 us
    unnamed x10, local copies, waits for them, and re-layouts  8.42 us

profile of v1, /device:TPU:161, one launch (start us, length us, event | category | flops | bytes accessed | tf_op | source)
XLA Modules:
  0.0 226.4 jit_solution(13261744954869658196)
XLA Ops:
  0.6 0.8 eq.34
  1.4 0.2 fusion
  1.6 0.1 convert_element_type.22
  1.7 0.7 multiply_add_fusion.1
  2.4 0.1 fusion.6
  2.4 0.9 select_reduce_fusion
  3.3 1.4 copy.14.gains_ref
  4.8 0.9 copy.13.slot_gain_ref
  5.6 0.2 iota_compare_fusion
  5.8 0.8 fusion.4.both_ref
  6.6 0.8 fusion.2
  7.4 212.0 %shard_map.110 = (bf16[160,2048]{1,0:T(8,128)(2,1)}, bf16[160,2048]{1,0:T(8,128)(2,1)}, bf16[1,128,768]{2,1,0:T(8,128)(2,1)}, bf16[1,128,768]{2,1,0:T(8,128)(2,1)}, bf16[1,128,768]{2,1,0:T(8,128)(2,1)}) custom-call(bf16[512,160]{1,0:T(8,128)(2,1)} %fusion.4.both_ref, bf16[160,512]{1,0:T(8,128)(2,1)} %get-tuple-element.7.first_ref, ...), custom_call_target="tpu_custom_call" | custom-call | tf_op jit(solution)/shard_map/pallas_call | solution.py:446
  219.4 0.0 copy-start.1
  219.4 0.0 copy-start
  219.4 2.0 copy.20
  221.5 2.0 copy.21
  223.4 1.6 copy.22
  225.1 0.0 copy-done.1
  225.1 0.7 copy.23
  225.7 0.0 copy-done
  225.7 0.7 copy.24
  (2 shorter events, 0.0 us)
Async XLA Ops:
  219.4 5.7 %copy-start.1 = (bf16[1,128,768]{2,1,0:T(8,128)(2,1)S(1)}, bf16[1,128,768]{2,1,0:T(8,128)(2,1)}, u32[]{:S(2)}) copy-start(bf16[1,128,768]{2,1,0:T(8,128)(2,1)} %get-tuple-element.17) | copy-start | bytes 589828
  219.4 6.3 %copy-start = (bf16[1,128,768]{2,1,0:T(8,128)(2,1)S(1)}, bf16[1,128,768]{2,1,0:T(8,128)(2,1)}, u32[]{:S(2)}) copy-start(bf16[1,128,768]{2,1,0:T(8,128)(2,1)} %get-tuple-element.18) | copy-start | bytes 589828

commit v2 on v1

--- a/solution.py
+++ b/solution.py
@@ -1,4 +1,5 @@
 import functools
+import math
 
 import jax
 import jax.numpy as jnp
@@ -10,26 +11,14 @@
 SLOTS = 32
 LANES = 128
 CHUNK = 256
-QUARTERS = 4
+QUARTERS = 8
 MESH = pl.DeviceIdType.MESH
+OFFSETS = (
+    (1, 0), (3, 0), (0, 1), (0, 3), (1, 1), (3, 3), (1, 3), (3, 1),
+    (2, 0), (0, 2), (2, 2), (2, 1), (1, 2), (2, 3), (3, 2),
+)
 F32 = jnp.float32
 BF16 = jnp.bfloat16
-
-
-def slot_masks(routes, experts):
-    rows, picks = routes.shape
-    total = rows * picks
-    chosen = routes.T.reshape(1, -1)
-    labels = lax.broadcasted_iota(jnp.int32, (experts, total), 0)
-    matches = chosen == labels
-    earlier = lax.broadcasted_iota(jnp.int32, (total, total), 0) < lax.broadcasted_iota(
-        jnp.int32, (total, total), 1
-    )
-    before = jnp.dot(matches.astype(BF16), earlier.astype(BF16), preferred_element_type=F32)
-    position = jnp.sum(jnp.where(matches, before, 0.0), axis=0).astype(jnp.int32)
-    target = (chosen[0] * SLOTS + position).reshape(picks, rows)
-    slots = lax.broadcasted_iota(jnp.int32, (picks, experts * SLOTS, rows), 1)
-    return slots == target[:, None, :], target
 
 
 def dot(a, b):
@@ -47,10 +36,7 @@
 def moe_kernel(
     n,
     nz,
-    both_ref,
-    first_ref,
-    second_ref,
-    slot_gain_ref,
+    routes_ref,
     gains_ref,
     tok_ref,
     cot_ref,
@@ -62,6 +48,8 @@
     gg_ref,
     gu_ref,
     gd_ref,
+    pick_a,
+    pick_b,
     w_buf,
     st,
     sc,
@@ -105,6 +93,12 @@
     mate = ex + sgn
     native = ex == d
     rootmate = mate == d
+    side = math.isqrt(n)
+    others = [
+        lax.rem(lax.div(d, side) + a, side) * side + lax.rem(lax.rem(d, side) + b, side)
+        for a, b in OFFSETS
+        if a < side and b < side
+    ]
 
     def remote(src, dst, send, recv, dev):
         return pltpu.make_async_remote_copy(
@@ -148,6 +142,30 @@
                         loc_sem.at[3 * k + m],
                     ).start()
 
+    count = tok_ref.shape[0]
+
+    def iota(shape, dim):
+        return lax.broadcasted_iota(jnp.int32, shape, dim)
+
+    def ones(mask):
+        return jnp.where(mask, 1.0, 0.0).astype(BF16)
+
+    names = [routes_ref[k : k + 1, :] for k in range(2)]
+    named = [name == iota((n, count), 0) for name in names]
+    square = (count, count)
+    before = dot(ones(named[0]) + ones(named[1]), ones(iota(square, 0) < iota(square, 1)))
+    for buf, name, match in zip((pick_a, pick_b), names, named):
+        place = jnp.sum(jnp.where(match, before, 0.0), axis=0, keepdims=True).astype(jnp.int32)
+        buf[...] = ones(iota((rows, count), 0) == name * SLOTS + place)
+    gain_a, gain_b = [
+        jnp.sum(
+            jnp.where(iota(square, 0) == iota(square, 1), gains_ref[k : k + 1, :], 0.0),
+            axis=1,
+            keepdims=True,
+        )
+        for k in range(2)
+    ]
+
     pl.semaphore_wait(
         barrier, n + 2 + jnp.where(d != ex, 1, 0) + jnp.where(rootmate, n - 1, 0)
     )
@@ -158,9 +176,7 @@
     def exchange(src, dst, send, recv, own):
         pltpu.make_async_copy(src.at[slot_rows(d)], dst.at[slot_rows(d)], one_sem.at[own]).start()
 
-        @pl.loop(1, n)
-        def _(j):
-            t = lax.rem(d + j, n)
+        for t in others:
             remote(
                 src.at[slot_rows(t)], dst.at[slot_rows(d)], one_sem.at[send], one_sem.at[recv], (t, ex)
             ).start()
@@ -175,37 +191,36 @@
     def piece(buf, k, m, q):
         return buf.at[k, m, pl.ds(pl.multiple_of(q * quarter, quarter), quarter)]
 
-    def weights(k):
-        @pl.loop(0, 3)
-        def _(m):
-            km = 3 * k + m
+    def weights(km):
+        k = lax.div(km, 3)
+        m = lax.rem(km, 3)
+
+        @pl.when(native)
+        def _():
+            wait_bytes(w_buf.at[:, k, m], loc_sem.at[km])
+
+        @pl.loop(0, QUARTERS)
+        def _(q):
+            i = QUARTERS * km + q
+            mine = piece(w_buf.at[c], k, m, q)
+
+            @pl.when(jnp.logical_not(native))
+            def _():
+                wait_bytes(mine, w_recv.at[i])
+
+            @pl.when(r <= nz - 2)
+            def _():
+                remote(mine, mine, one_sem.at[WS], w_recv.at[i], (d, nxt)).start()
 
             @pl.when(native)
             def _():
-                wait_bytes(w_buf.at[:, k, m], loc_sem.at[km])
-
-            @pl.loop(0, QUARTERS)
-            def _(q):
-                i = QUARTERS * km + q
-                mine = piece(w_buf.at[c], k, m, q)
-
-                @pl.when(jnp.logical_not(native))
-                def _():
-                    wait_bytes(mine, w_recv.at[i])
-
-                @pl.when(r <= nz - 2)
-                def _():
-                    remote(mine, mine, one_sem.at[WS], w_recv.at[i], (d, nxt)).start()
-
-                @pl.when(native)
-                def _():
-                    other = piece(w_buf.at[1 - c], k, m, q)
-                    remote(other, other, one_sem.at[PS], w_recv.at[i], (d, mate)).start()
-
-            @pl.when(jnp.logical_not(rootmate))
-            def _():
-                half = w_buf.at[c, k, m]
-                remote(half, half, one_sem.at[XS], x_recv.at[km], (d, mate)).start()
+                other = piece(w_buf.at[1 - c], k, m, q)
+                remote(other, other, one_sem.at[PS], w_recv.at[i], (d, mate)).start()
+
+        @pl.when(jnp.logical_not(rootmate))
+        def _():
+            half = w_buf.at[c, k, m]
+            remote(half, half, one_sem.at[XS], x_recv.at[km], (d, mate)).start()
 
     def swapped(k):
         @pl.when(jnp.logical_not(native))
@@ -270,101 +285,124 @@
                 acc += dot_rows(dup[k], rows_of(k, 1, sl))
             pg[:, sl] = acc.astype(BF16)
 
-    def chain(k):
-        wait_bytes(dx_buf.at[k], dx_recv.at[k])
-
-        @pl.loop(0, 3)
-        def _(m):
-            km = 3 * k + m
-
-            @pl.loop(0, QUARTERS)
-            def _(q):
-                i = QUARTERS * km + q
-                sl = pl.ds(pl.multiple_of(q * quarter, quarter), quarter)
-                mine = piece(dpart.at[c], k, m, q)
-                there = piece(ch_buf, k, m, q)
-                own = dpart[c, k, m, sl, :].astype(F32) + dx_buf[k, m, sl, :].astype(F32)
-
-                @pl.when(r == 1)
-                def _():
-                    dpart[c, k, m, sl, :] = own.astype(BF16)
-
-                @pl.when(r != 1)
-                def _():
-                    wait_bytes(there, ch_recv.at[i])
-                    dpart[c, k, m, sl, :] = (own + ch_buf[k, m, sl, :].astype(F32)).astype(BF16)
-
-                @pl.when(r != 0)
-                def _():
-                    remote(mine, there, one_sem.at[HS], ch_recv.at[i], (d, nxt)).start()
-
-            @pl.when(r == 0)
-            def _():
-                def share(t):
-                    return dpart.at[c, k, m, pl.ds(pl.multiple_of(t * depth, depth), depth)]
-
-                @pl.when(native)
-                def _():
-                    pltpu.make_async_copy(share(d), fg.at[c, k, m], one_sem.at[FL]).start()
-
-                @pl.when(rootmate)
-                def _():
-                    remote(
-                        share(d), fg.at[c, k, m], one_sem.at[FS], one_sem.at[FR], (d, d)
-                    ).start()
-
-                @pl.loop(1, n)
-                def _(j):
-                    t = lax.rem(d + j, n)
-                    remote(
-                        share(t), fg.at[c, k, m], one_sem.at[FS], one_sem.at[FR], (t, d)
-                    ).start()
+    def chain(k, m):
+        if m == 0:
+            wait_bytes(dx_buf.at[k], dx_recv.at[k])
+        km = 3 * k + m
+
+        @pl.loop(0, QUARTERS)
+        def _(q):
+            i = QUARTERS * km + q
+            sl = pl.ds(pl.multiple_of(q * quarter, quarter), quarter)
+            mine = piece(dpart.at[c], k, m, q)
+            there = piece(ch_buf, k, m, q)
+            own = dpart[c, k, m, sl, :].astype(F32) + dx_buf[k, m, sl, :].astype(F32)
+
+            @pl.when(r == 1)
+            def _():
+                dpart[c, k, m, sl, :] = own.astype(BF16)
+
+            @pl.when(r != 1)
+            def _():
+                wait_bytes(there, ch_recv.at[i])
+                dpart[c, k, m, sl, :] = (own + ch_buf[k, m, sl, :].astype(F32)).astype(BF16)
+
+            @pl.when(r != 0)
+            def _():
+                remote(mine, there, one_sem.at[HS], ch_recv.at[i], (d, nxt)).start()
+
+        @pl.when(r == 0)
+        def _():
+            def share(t):
+                return dpart.at[c, k, m, pl.ds(pl.multiple_of(t * depth, depth), depth)]
+
+            @pl.when(native)
+            def _():
+                pltpu.make_async_copy(share(d), fg.at[c, k, m], one_sem.at[FL]).start()
+
+            @pl.when(rootmate)
+            def _():
+                remote(share(d), fg.at[c, k, m], one_sem.at[FS], one_sem.at[FR], (d, d)).start()
+
+            for t in others:
+                remote(share(t), fg.at[c, k, m], one_sem.at[FS], one_sem.at[FR], (t, d)).start()
 
     @pl.loop(0, width // 512)
     def _(i):
         sl = cols(i, 512)
-        st[:, sl] = dot(both_ref[...], tok_ref[:, sl]).astype(BF16)
+        st[:, sl] = dot(pick_a[...] + pick_b[...], tok_ref[:, sl]).astype(BF16)
 
     exchange(st, x_buf, TS, TR, TL)
 
     @pl.loop(0, width // 512)
     def _(i):
         sl = cols(i, 512)
-        sc[:, sl] = (slot_gain_ref[...] * dot(both_ref[...], cot_ref[:, sl])).astype(BF16)
+        cot = cot_ref[:, sl].astype(F32)
+        sc[:, sl] = (
+            dot(pick_a[...], (gain_a * cot).astype(BF16))
+            + dot(pick_b[...], (gain_b * cot).astype(BF16))
+        ).astype(BF16)
 
     exchange(sc, c_buf, CS, CR, CL)
 
-    @pl.loop(0, chunks)
-    def _(k):
-        weights(k)
+    middle = nz // 2
+    early = r < middle
+    late = jnp.logical_not(early)
+    near = jnp.logical_and(r >= 1, r < middle)
+    mid = jnp.logical_and(r >= middle, r <= middle + 1)
+    far = jnp.logical_or(r == 0, r > middle + 1)
+
+    @pl.loop(0, 6)
+    def _(km):
+        weights(km)
+
+    @pl.when(early)
+    def _():
+        @pl.loop(6, 9)
+        def _(km):
+            weights(km)
 
     exchanged(x_buf, TR, TL)
     exchanged(c_buf, CR, CL)
-
-    @pl.loop(0, chunks)
-    def _(k):
-        swapped(k)
-        hidden_units(k)
-        outer(k)
-
+    swapped(0)
+    hidden_units(0)
+    pl.when(late)(lambda: weights(6))
+    outer(0)
+    pl.when(late)(lambda: weights(7))
+    swapped(1)
+    hidden_units(1)
+    pl.when(late)(lambda: weights(8))
+    outer(1)
+    pl.when(near)(lambda: chain(0, 0))
+    swapped(2)
+    hidden_units(2)
+    pl.when(near)(lambda: chain(0, 1))
     produce()
     exchange(po, bo, OS, OR, OL)
+    pl.when(mid)(lambda: chain(0, 0))
     pick_grads()
     exchange(pg, bg, GS, GR, GL)
-
-    @pl.loop(0, chunks)
-    def _(k):
-        chain(k)
+    pl.when(mid)(lambda: chain(0, 1))
+
+    @pl.when(far)
+    def _():
+        chain(0, 0)
+        chain(0, 1)
+
+    chain(0, 2)
+    outer(2)
+    for k in range(1, chunks):
+        for m in range(3):
+            chain(k, m)
 
     exchanged(bo, OR, OL)
-    gain = gains_ref[...]
 
     @pl.loop(0, width // 512)
     def _(i):
         sl = cols(i, 512)
         got = bo[:, sl]
         out_ref[:, sl] = (
-            gain[:, 0:1] * dot(first_ref[...], got) + gain[:, 1:2] * dot(second_ref[...], got)
+            gain_a * dot_outer(pick_a[...], got) + gain_b * dot_outer(pick_b[...], got)
         ).astype(BF16)
 
     exchanged(bg, GR, GL)
@@ -373,7 +411,9 @@
     def _(i):
         sl = cols(i, 512)
         got = bg[:, sl]
-        ingrad_ref[:, sl] = (dot(first_ref[...], got) + dot(second_ref[...], got)).astype(BF16)
+        ingrad_ref[:, sl] = (
+            dot_outer(pick_a[...], got) + dot_outer(pick_b[...], got)
+        ).astype(BF16)
 
     @pl.when(native)
     def _():
@@ -425,14 +465,6 @@
     count = tokens.shape[0]
     depth = width // n
     rows = n * SLOTS
-
-    masks, target = slot_masks(routes, n)
-    both = (masks[0] | masks[1]).astype(BF16)
-    gains = route_gains.T
-    slot_gain = jnp.sum(jnp.where(masks, gains[:, None, :], 0.0), axis=(0, 2))[:, None]
-    slots = lax.broadcasted_iota(jnp.int32, (count, rows), 1)
-    first = (slots == target[0][:, None]).astype(BF16)
-    second = (slots == target[1][:, None]).astype(BF16)
 
     vmem = pl.BlockSpec(memory_space=pltpu.VMEM)
     anywhere = pl.BlockSpec(memory_space=pl.ANY)
@@ -446,9 +478,11 @@
     return pl.pallas_call(
         functools.partial(moe_kernel, n, n // 2),
         out_shape=(row_out, row_out, share, share, share),
-        in_specs=[vmem] * 7 + [anywhere] * 3,
+        in_specs=[vmem] * 4 + [anywhere] * 3,
         out_specs=(vmem,) * 5,
         scratch_shapes=[
+            pltpu.VMEM((rows, count), BF16),
+            pltpu.VMEM((rows, count), BF16),
             halves,
             landed,
             landed,
@@ -475,7 +509,7 @@
         compiler_params=pltpu.CompilerParams(
             collective_id=0, has_side_effects=True, vmem_limit_bytes=60 * 2**20
         ),
-    )(both, first, second, slot_gain, route_gains, tokens, cotangent, w_gate, w_up, w_down)
+    )(routes.T, route_gains.T, tokens, cotangent, w_gate, w_up, w_down)
 
 
 def solution(mesh):

time: 227 us -> 198 us (0.87)
  the two profiles are of different devices: /device:TPU:161 before, /device:TPU:105 now
where the time goes in v2:
time: 198 us; the launch traced here: 196 us
  Pallas kernels  188 us (95%)
  local copies, waits for them, and re-layouts  6.99 us (4%)
    pallas_call x1, Pallas kernels, shards(): pl.pallas_call(functools.partial(moe_kernel, n, n // 2), out_shape=(row_o...  188 us
    unnamed x9, local copies, waits for them, and re-layouts  6.99 us

profile of v2, /device:TPU:105, one launch (start us, length us, event | category | flops | bytes accessed | tf_op | source)
XLA Modules:
  0.0 195.6 jit_solution(1208446530102469915)
XLA Ops:
  0.6 187.9 %shard_map.110 = (bf16[160,2048]{1,0:T(8,128)(2,1)}, bf16[160,2048]{1,0:T(8,128)(2,1)}, bf16[1,128,768]{2,1,0:T(8,128)(2,1)}, bf16[1,128,768]{2,1,0:T(8,128)(2,1)}, bf16[1,128,768]{2,1,0:T(8,128)(2,1)}) custom-call(s32[2,160]{1,0:T(2,128)} %bitcast.2, f32[2,160]{1,0:T(2,128)} %bitcast.3, bf16[160,2048]{1,0:T(8,128)(2,1)} %tok_ref.1, ...), custom_call_target="tpu_custom_call" | custom-call | tf_op jit(solution)/shard_map/pallas_call | solution.py:478
  188.6 0.0 copy-start.1
  188.6 0.0 copy-start
  188.6 2.0 %copy.17 = bf16[160,2048]{1,0:T(8,128)(2,1)} copy(bf16[160,2048]{1,0:T(8,128)(2,1)} %get-tuple-element.10) | data formatting | bytes 1310720
  190.6 2.0 %copy.18 = bf16[160,2048]{1,0:T(8,128)(2,1)} copy(bf16[160,2048]{1,0:T(8,128)(2,1)} %get-tuple-element.11) | data formatting | bytes 1310720
  192.6 1.6 copy.19
  194.2 0.0 copy-done.1
  194.2 0.7 copy.20
  194.9 0.0 copy-done
  194.9 0.7 copy.21
Async XLA Ops:
  188.6 5.7 %copy-start.1 = (bf16[1,128,768]{2,1,0:T(8,128)(2,1)S(1)}, bf16[1,128,768]{2,1,0:T(8,128)(2,1)}, u32[]{:S(2)}) copy-start(bf16[1,128,768]{2,1,0:T(8,128)(2,1)} %get-tuple-element.13) | copy-start | bytes 589828
  188.6 6.3 %copy-start = (bf16[1,128,768]{2,1,0:T(8,128)(2,1)S(1)}, bf16[1,128,768]{2,1,0:T(8,128)(2,1)}, u32[]{:S(2)}) copy-start(bf16[1,128,768]{2,1,0:T(8,128)(2,1)} %get-tuple-element.14) | copy-start | bytes 589828

commit v3 on v2

--- a/solution.py
+++ b/solution.py
@@ -285,10 +285,13 @@
                 acc += dot_rows(dup[k], rows_of(k, 1, sl))
             pg[:, sl] = acc.astype(BF16)
 
-    def chain(k, m):
-        if m == 0:
+    def chain(km):
+        k = lax.div(km, 3)
+        m = lax.rem(km, 3)
+
+        @pl.when(m == 0)
+        def _():
             wait_bytes(dx_buf.at[k], dx_recv.at[k])
-        km = 3 * k + m
 
         @pl.loop(0, QUARTERS)
         def _(q):
@@ -348,9 +351,14 @@
     middle = nz // 2
     early = r < middle
     late = jnp.logical_not(early)
-    near = jnp.logical_and(r >= 1, r < middle)
-    mid = jnp.logical_and(r >= middle, r <= middle + 1)
-    far = jnp.logical_or(r == 0, r > middle + 1)
+
+    def groups(first, second, third):
+        return jnp.where(r == 1, first, jnp.where(r == 2, second, jnp.where(r == 3, third, 0)))
+
+    def sums(start, stop):
+        @pl.loop(start, stop)
+        def _(km):
+            chain(km)
 
     @pl.loop(0, 6)
     def _(km):
@@ -373,27 +381,18 @@
     hidden_units(1)
     pl.when(late)(lambda: weights(8))
     outer(1)
-    pl.when(near)(lambda: chain(0, 0))
+    sums(0, groups(3, 0, 0))
     swapped(2)
     hidden_units(2)
-    pl.when(near)(lambda: chain(0, 1))
+    sums(groups(3, 0, 0), groups(4, 0, 0))
     produce()
     exchange(po, bo, OS, OR, OL)
-    pl.when(mid)(lambda: chain(0, 0))
+    sums(groups(4, 0, 0), groups(5, 2, 1))
     pick_grads()
     exchange(pg, bg, GS, GR, GL)
-    pl.when(mid)(lambda: chain(0, 1))
-
-    @pl.when(far)
-    def _():
-        chain(0, 0)
-        chain(0, 1)
-
-    chain(0, 2)
+    sums(groups(5, 2, 1), groups(6, 3, 2))
     outer(2)
-    for k in range(1, chunks):
-        for m in range(3):
-            chain(k, m)
+    sums(groups(6, 3, 2), 9)
 
     exchanged(bo, OR, OL)
 

time: 198 us -> 187 us (0.944); the launches traced: 196 us -> 187 us
  Pallas kernels: 188 us -> 179 us
    pallas_call x1, Pallas kernels: 188 us -> 179 us  [shards(): pl.pallas_call(functools.partial(moe_kernel, n, n // 2), out_shape=(row_o...]
where the time goes in v3:
time: 187 us
  Pallas kernels  179 us (96%)
  local copies, waits for them, and re-layouts  6.99 us (4%)
    pallas_call x1, Pallas kernels, shards(): pl.pallas_call(functools.partial(moe_kernel, n, n // 2), out_shape=(row_o...  179 us
    unnamed x9, local copies, waits for them, and re-layouts  6.99 us

profile of v3, /device:TPU:105, one launch (start us, length us, event | category | flops | bytes accessed | tf_op | source)
XLA Modules:
  0.0 187.0 jit_solution(1994566492673249305)
XLA Ops:
  0.6 179.4 %shard_map.110 = (bf16[160,2048]{1,0:T(8,128)(2,1)}, bf16[160,2048]{1,0:T(8,128)(2,1)}, bf16[1,128,768]{2,1,0:T(8,128)(2,1)}, bf16[1,128,768]{2,1,0:T(8,128)(2,1)}, bf16[1,128,768]{2,1,0:T(8,128)(2,1)}) custom-call(s32[2,160]{1,0:T(2,128)} %bitcast.2, f32[2,160]{1,0:T(2,128)} %bitcast.3, bf16[160,2048]{1,0:T(8,128)(2,1)} %tok_ref.1, ...), custom_call_target="tpu_custom_call" | custom-call | tf_op jit(solution)/shard_map/pallas_call | solution.py:477
  180.0 0.0 copy-start.1
  180.0 0.0 copy-start
  180.0 2.0 %copy.17 = bf16[160,2048]{1,0:T(8,128)(2,1)} copy(bf16[160,2048]{1,0:T(8,128)(2,1)} %get-tuple-element.10) | data formatting | bytes 1310720
  182.1 2.0 %copy.18 = bf16[160,2048]{1,0:T(8,128)(2,1)} copy(bf16[160,2048]{1,0:T(8,128)(2,1)} %get-tuple-element.11) | data formatting | bytes 1310720
  184.0 1.6 copy.19
  185.7 0.0 copy-done.1
  185.7 0.7 copy.20
  186.3 0.0 copy-done
  186.3 0.7 copy.21
Async XLA Ops:
  180.0 5.7 %copy-start.1 = (bf16[1,128,768]{2,1,0:T(8,128)(2,1)S(1)}, bf16[1,128,768]{2,1,0:T(8,128)(2,1)}, u32[]{:S(2)}) copy-start(bf16[1,128,768]{2,1,0:T(8,128)(2,1)} %get-tuple-element.13) | copy-start | bytes 589828
  180.0 6.3 %copy-start = (bf16[1,128,768]{2,1,0:T(8,128)(2,1)S(1)}, bf16[1,128,768]{2,1,0:T(8,128)(2,1)}, u32[]{:S(2)}) copy-start(bf16[1,128,768]{2,1,0:T(8,128)(2,1)} %get-tuple-element.14) | copy-start | bytes 589828

commit v4 on v3

--- a/solution.py
+++ b/solution.py
@@ -260,7 +260,10 @@
             dpart[0, k, 2, sl, :] = down[:, :LANES]
             dpart[1, k, 2, sl, :] = down[:, LANES:]
 
-        remote(dpart.at[1 - c, k], dx_buf.at[k], one_sem.at[DS], dx_recv.at[k], (d, mate)).start()
+        for m in range(3):
+            remote(
+                dpart.at[1 - c, k, m], dx_buf.at[k, m], one_sem.at[DS], dx_recv.at[3 * k + m], (d, mate)
+            ).start()
 
     def rows_of(k, m, sl):
         return jnp.concatenate([w_buf[0, k, m, sl, :], w_buf[1, k, m, sl, :]], axis=1)
@@ -289,9 +292,7 @@
         k = lax.div(km, 3)
         m = lax.rem(km, 3)
 
-        @pl.when(m == 0)
-        def _():
-            wait_bytes(dx_buf.at[k], dx_recv.at[k])
+        wait_bytes(dx_buf.at[k, m], dx_recv.at[km])
 
         @pl.loop(0, QUARTERS)
         def _(q):
@@ -457,6 +458,15 @@
     wait_bytes(dx_buf, one_sem.at[DS])
 
 
+def hand_over(*refs):
+    sems = refs[10]
+    copies = [pltpu.make_async_copy(refs[i], refs[5 + i], sems.at[i]) for i in range(5)]
+    for copy in copies:
+        copy.start()
+    for copy in copies:
+        copy.wait()
+
+
 def shards(n, tokens, routes, route_gains, cotangent, w_gate, w_up, w_down):
     width = tokens.shape[1]
     units = w_gate.shape[2]
@@ -474,7 +484,7 @@
     acts = pltpu.VMEM((chunks, rows, CHUNK), BF16)
     half = pltpu.VMEM((chunks, 3, width, LANES), BF16)
     halves = pltpu.VMEM((2, chunks, 3, width, LANES), BF16)
-    return pl.pallas_call(
+    results = pl.pallas_call(
         functools.partial(moe_kernel, n, n // 2),
         out_shape=(row_out, row_out, share, share, share),
         in_specs=[vmem] * 4 + [anywhere] * 3,
@@ -502,13 +512,20 @@
             sem((3 * chunks * QUARTERS,)),
             sem((3 * chunks,)),
             sem((3 * chunks * QUARTERS,)),
-            sem((chunks,)),
+            sem((3 * chunks,)),
             sem((20,)),
         ],
         compiler_params=pltpu.CompilerParams(
             collective_id=0, has_side_effects=True, vmem_limit_bytes=60 * 2**20
         ),
     )(routes.T, route_gains.T, tokens, cotangent, w_gate, w_up, w_down)
+    return pl.pallas_call(
+        hand_over,
+        out_shape=(row_out, row_out, share, share, share),
+        in_specs=[anywhere] * 5,
+        out_specs=(anywhere,) * 5,
+        scratch_shapes=[sem((5,))],
+    )(*results)
 
 
 def solution(mesh):

time: 187 us -> 239 us (1.28)
  Pallas kernels: 179 us -> 238 us
  local copies, waits for them, and re-layouts: 6.99 us -> 0 us
    pallas_call x0 -> x1, Pallas kernels: none -> 58.7 us  [shards(): pl.pallas_call(hand_over, out_shape=(row_out, row_out, share, share, shar...]
    unnamed x9 -> x0, local copies, waits for them, and re-layouts: 6.99 us -> none
where the time goes in v4:
time: 239 us
  Pallas kernels  238 us (100%)
    pallas_call x1, Pallas kernels, shards(): pl.pallas_call(functools.partial(moe_kernel, n, n // 2), out_shape=(row_o...  179 us
    pallas_call x1, Pallas kernels, shards(): pl.pallas_call(hand_over, out_shape=(row_out, row_out, share, share, shar...  58.7 us

profile of v4, /device:TPU:105, one launch (start us, length us, event | category | flops | bytes accessed | tf_op | source)
XLA Modules:
  0.0 238.8 jit_solution(17635081355806373217)
XLA Ops:
  0.6 179.4 %shard_map.110 = (bf16[160,2048]{1,0:T(8,128)(2,1)}, bf16[160,2048]{1,0:T(8,128)(2,1)}, bf16[1,128,768]{2,1,0:T(8,128)(2,1)}, bf16[1,128,768]{2,1,0:T(8,128)(2,1)}, bf16[1,128,768]{2,1,0:T(8,128)(2,1)}) custom-call(s32[2,160]{1,0:T(2,128)} %bitcast.2, f32[2,160]{1,0:T(2,128)} %bitcast.3, bf16[160,2048]{1,0:T(8,128)(2,1)} %tok_ref.1, ...), custom_call_target="tpu_custom_call" | custom-call | tf_op jit(solution)/shard_map/pallas_call | solution.py:487
  180.1 58.7 %shard_map.111 = (bf16[160,2048]{1,0:T(8,128)(2,1)}, bf16[160,2048]{1,0:T(8,128)(2,1)}, bf16[1,128,768]{2,1,0:T(8,128)(2,1)}, bf16[1,128,768]{2,1,0:T(8,128)(2,1)}, bf16[1,128,768]{2,1,0:T(8,128)(2,1)}) custom-call(bf16[160,2048]{1,0:T(8,128)(2,1)} %get-tuple-element.10.refs_0_, bf16[160,2048]{1,0:T(8,128)(2,1)} %get-tuple-element.11.refs_1_, ...), custom_call_target="tpu_custom_call" | custom-call | tf_op jit(solution)/shard_map/pallas_call | solution.py:522

commit v5 on v4

--- a/solution.py
+++ b/solution.py
@@ -12,6 +12,8 @@
 LANES = 128
 CHUNK = 256
 QUARTERS = 8
+AHEAD = 4
+SUMS_AHEAD = 24
 MESH = pl.DeviceIdType.MESH
 OFFSETS = (
     (1, 0), (3, 0), (0, 1), (0, 3), (1, 1), (3, 3), (1, 3), (3, 1),
@@ -71,6 +73,8 @@
     x_recv,
     ch_recv,
     dx_recv,
+    w_send,
+    ch_send,
     one_sem,
 ):
     (TS, TR, TL, CS, CR, CL, OS, OR, OL, GS, GR, GL, WS, PS, XS, HS, DS, FS, FR, FL) = range(20)
@@ -210,7 +214,13 @@
 
             @pl.when(r <= nz - 2)
             def _():
-                remote(mine, mine, one_sem.at[WS], w_recv.at[i], (d, nxt)).start()
+                slot = w_send.at[lax.rem(i, AHEAD)]
+
+                @pl.when(i >= AHEAD)
+                def _():
+                    wait_bytes(mine, slot)
+
+                remote(mine, mine, slot, w_recv.at[i], (d, nxt)).start()
 
             @pl.when(native)
             def _():
@@ -313,7 +323,13 @@
 
             @pl.when(r != 0)
             def _():
-                remote(mine, there, one_sem.at[HS], ch_recv.at[i], (d, nxt)).start()
+                slot = ch_send.at[lax.rem(i, SUMS_AHEAD)]
+
+                @pl.when(i >= SUMS_AHEAD)
+                def _():
+                    wait_bytes(mine, slot)
+
+                remote(mine, there, slot, ch_recv.at[i], (d, nxt)).start()
 
         @pl.when(r == 0)
         def _():
@@ -441,7 +457,9 @@
 
     @pl.when(r <= nz - 2)
     def _():
-        wait_bytes(w_buf.at[0], one_sem.at[WS])
+        @pl.loop(0, AHEAD)
+        def _(i):
+            wait_bytes(w_buf.at[0, 0, 0, pl.ds(0, quarter)], w_send.at[i])
 
     @pl.when(native)
     def _():
@@ -453,18 +471,16 @@
 
     @pl.when(r != 0)
     def _():
-        wait_bytes(ch_buf, one_sem.at[HS])
+        @pl.loop(0, SUMS_AHEAD)
+        def _(i):
+            wait_bytes(ch_buf.at[0, 0, pl.ds(0, quarter)], ch_send.at[i])
 
     wait_bytes(dx_buf, one_sem.at[DS])
 
 
 def hand_over(*refs):
-    sems = refs[10]
-    copies = [pltpu.make_async_copy(refs[i], refs[5 + i], sems.at[i]) for i in range(5)]
-    for copy in copies:
-        copy.start()
-    for copy in copies:
-        copy.wait()
+    for i in range(5):
+        refs[5 + i][...] = refs[i][...]
 
 
 def shards(n, tokens, routes, route_gains, cotangent, w_gate, w_up, w_down):
@@ -513,6 +529,8 @@
             sem((3 * chunks,)),
             sem((3 * chunks * QUARTERS,)),
             sem((3 * chunks,)),
+            sem((AHEAD,)),
+            sem((SUMS_AHEAD,)),
             sem((20,)),
         ],
         compiler_params=pltpu.CompilerParams(
@@ -522,9 +540,8 @@
     return pl.pallas_call(
         hand_over,
         out_shape=(row_out, row_out, share, share, share),
-        in_specs=[anywhere] * 5,
-        out_specs=(anywhere,) * 5,
-        scratch_shapes=[sem((5,))],
+        in_specs=[vmem] * 5,
+        out_specs=(vmem,) * 5,
     )(*results)
 
 

time: 239 us -> 190 us (0.79)
  the two profiles are of different devices: /device:TPU:105 before, /device:TPU:152 now
where the time goes in v5:
time: 190 us
  Pallas kernels  190 us (100%)
    pallas_call x1, Pallas kernels, shards(): pl.pallas_call(functools.partial(moe_kernel, n, n // 2), out_shape=(row_o...  187 us

profile of v5, /device:TPU:152, one launch (start us, length us, event | category | flops | bytes accessed | tf_op | source)
XLA Modules:
  0.0 190.2 jit_solution(9177221301282771003)
XLA Ops:
  0.6 186.8 %shard_map.110 = (bf16[160,2048]{1,0:T(8,128)(2,1)}, bf16[160,2048]{1,0:T(8,128)(2,1)}, bf16[1,128,768]{2,1,0:T(8,128)(2,1)}, bf16[1,128,768]{2,1,0:T(8,128)(2,1)}, bf16[1,128,768]{2,1,0:T(8,128)(2,1)}) custom-call(s32[2,160]{1,0:T(2,128)} %bitcast.2, f32[2,160]{1,0:T(2,128)} %bitcast.3, bf16[160,2048]{1,0:T(8,128)(2,1)} %tok_ref.1, ...), custom_call_target="tpu_custom_call" | custom-call | tf_op jit(solution)/shard_map/pallas_call | solution.py:503
  187.5 2.7 %shard_map.111 = (bf16[160,2048]{1,0:T(8,128)(2,1)}, bf16[160,2048]{1,0:T(8,128)(2,1)}, bf16[1,128,768]{2,1,0:T(8,128)(2,1)}, bf16[1,128,768]{2,1,0:T(8,128)(2,1)}, bf16[1,128,768]{2,1,0:T(8,128)(2,1)}) custom-call(bf16[160,2048]{1,0:T(8,128)(2,1)} %get-tuple-element.10.refs_0_, bf16[160,2048]{1,0:T(8,128)(2,1)} %get-tuple-element.11.refs_1_, ...), custom_call_target="tpu_custom_call" | custom-call | tf_op jit(solution)/shard_map/pallas_call | solution.py:540

commit v6 on v4

--- a/solution.py
+++ b/solution.py
@@ -393,27 +393,32 @@
     exchange(pg, bg, GS, GR, GL)
     sums(groups(5, 2, 1), groups(6, 3, 2))
     outer(2)
-    sums(groups(6, 3, 2), 9)
-
-    exchanged(bo, OR, OL)
-
-    @pl.loop(0, width // 512)
-    def _(i):
-        sl = cols(i, 512)
-        got = bo[:, sl]
-        out_ref[:, sl] = (
-            gain_a * dot_outer(pick_a[...], got) + gain_b * dot_outer(pick_b[...], got)
-        ).astype(BF16)
-
-    exchanged(bg, GR, GL)
-
-    @pl.loop(0, width // 512)
-    def _(i):
-        sl = cols(i, 512)
-        got = bg[:, sl]
-        ingrad_ref[:, sl] = (
-            dot_outer(pick_a[...], got) + dot_outer(pick_b[...], got)
-        ).astype(BF16)
+    def finish_rows():
+        exchanged(bo, OR, OL)
+
+        @pl.loop(0, width // 512)
+        def _(i):
+            sl = cols(i, 512)
+            got = bo[:, sl]
+            out_ref[:, sl] = (
+                gain_a * dot_outer(pick_a[...], got) + gain_b * dot_outer(pick_b[...], got)
+            ).astype(BF16)
+
+        exchanged(bg, GR, GL)
+
+        @pl.loop(0, width // 512)
+        def _(i):
+            sl = cols(i, 512)
+            got = bg[:, sl]
+            ingrad_ref[:, sl] = (
+                dot_outer(pick_a[...], got) + dot_outer(pick_b[...], got)
+            ).astype(BF16)
+
+    last = jnp.logical_or(r == 0, r >= nz - 3)
+    sums(groups(6, 3, 2), 8)
+    pl.when(last)(finish_rows)
+    sums(8, 9)
+    pl.when(jnp.logical_not(last))(finish_rows)
 
     @pl.when(native)
     def _():
@@ -459,12 +464,8 @@
 
 
 def hand_over(*refs):
-    sems = refs[10]
-    copies = [pltpu.make_async_copy(refs[i], refs[5 + i], sems.at[i]) for i in range(5)]
-    for copy in copies:
-        copy.start()
-    for copy in copies:
-        copy.wait()
+    for i in range(5):
+        refs[5 + i][...] = refs[i][...]
 
 
 def shards(n, tokens, routes, route_gains, cotangent, w_gate, w_up, w_down):
@@ -522,9 +523,8 @@
     return pl.pallas_call(
         hand_over,
         out_shape=(row_out, row_out, share, share, share),
-        in_specs=[anywhere] * 5,
-        out_specs=(anywhere,) * 5,
-        scratch_shapes=[sem((5,))],
+        in_specs=[vmem] * 5,
+        out_specs=(vmem,) * 5,
     )(*results)
 
 

time: 239 us -> 185 us (0.77)
  Pallas kernels: 238 us -> 184 us
    pallas_call x1, Pallas kernels: 58.7 us -> 2.72 us  [shards(): pl.pallas_call(hand_over, out_shape=(row_out, row_out, share, share, shar...]
where the time goes in v6:
time: 185 us
  Pallas kernels  184 us (99%)
    pallas_call x1, Pallas kernels, shards(): pl.pallas_call(functools.partial(moe_kernel, n, n // 2), out_shape=(row_o...  181 us

profile of v6, /device:TPU:105, one launch (start us, length us, event | category | flops | bytes accessed | tf_op | source)
XLA Modules:
  0.0 184.6 jit_solution(10442099709419053480)
XLA Ops:
  0.6 181.3 %shard_map.110 = (bf16[160,2048]{1,0:T(8,128)(2,1)}, bf16[160,2048]{1,0:T(8,128)(2,1)}, bf16[1,128,768]{2,1,0:T(8,128)(2,1)}, bf16[1,128,768]{2,1,0:T(8,128)(2,1)}, bf16[1,128,768]{2,1,0:T(8,128)(2,1)}) custom-call(s32[2,160]{1,0:T(2,128)} %bitcast.2, f32[2,160]{1,0:T(2,128)} %bitcast.3, bf16[160,2048]{1,0:T(8,128)(2,1)} %tok_ref.1, ...), custom_call_target="tpu_custom_call" | custom-call | tf_op jit(solution)/shard_map/pallas_call | solution.py:488
  181.9 2.7 %shard_map.111 = (bf16[160,2048]{1,0:T(8,128)(2,1)}, bf16[160,2048]{1,0:T(8,128)(2,1)}, bf16[1,128,768]{2,1,0:T(8,128)(2,1)}, bf16[1,128,768]{2,1,0:T(8,128)(2,1)}, bf16[1,128,768]{2,1,0:T(8,128)(2,1)}) custom-call(bf16[160,2048]{1,0:T(8,128)(2,1)} %get-tuple-element.10.refs_0_, bf16[160,2048]{1,0:T(8,128)(2,1)} %get-tuple-element.11.refs_1_, ...), custom_call_target="tpu_custom_call" | custom-call | tf_op jit(solution)/shard_map/pallas_call | solution.py:523

commit v7 on v6

--- a/solution.py
+++ b/solution.py
@@ -331,12 +331,15 @@
             for t in others:
                 remote(share(t), fg.at[c, k, m], one_sem.at[FS], one_sem.at[FR], (t, d)).start()
 
+    pl.when(native)(lambda: weights(0))
+
     @pl.loop(0, width // 512)
     def _(i):
         sl = cols(i, 512)
         st[:, sl] = dot(pick_a[...] + pick_b[...], tok_ref[:, sl]).astype(BF16)
 
     exchange(st, x_buf, TS, TR, TL)
+    pl.when(native)(lambda: weights(1))
 
     @pl.loop(0, width // 512)
     def _(i):
@@ -361,7 +364,7 @@
         def _(km):
             chain(km)
 
-    @pl.loop(0, 6)
+    @pl.loop(jnp.where(native, 2, 0), 6)
     def _(km):
         weights(km)
 

time: 185 us -> 185 us (level)
  no operation moved by 1% of the time
where the time goes in v7:
time: 185 us
  Pallas kernels  184 us (99%)
    pallas_call x1, Pallas kernels, shards(): pl.pallas_call(functools.partial(moe_kernel, n, n // 2), out_shape=(row_o...  182 us

profile of v7, /device:TPU:105, one launch (start us, length us, event | category | flops | bytes accessed | tf_op | source)
XLA Modules:
  0.0 184.9 jit_solution(5529827817722486966)
XLA Ops:
  0.6 181.5 %shard_map.110 = (bf16[160,2048]{1,0:T(8,128)(2,1)}, bf16[160,2048]{1,0:T(8,128)(2,1)}, bf16[1,128,768]{2,1,0:T(8,128)(2,1)}, bf16[1,128,768]{2,1,0:T(8,128)(2,1)}, bf16[1,128,768]{2,1,0:T(8,128)(2,1)}) custom-call(s32[2,160]{1,0:T(2,128)} %bitcast.2, f32[2,160]{1,0:T(2,128)} %bitcast.3, bf16[160,2048]{1,0:T(8,128)(2,1)} %tok_ref.1, ...), custom_call_target="tpu_custom_call" | custom-call | tf_op jit(solution)/shard_map/pallas_call | solution.py:491
  182.2 2.7 %shard_map.111 = (bf16[160,2048]{1,0:T(8,128)(2,1)}, bf16[160,2048]{1,0:T(8,128)(2,1)}, bf16[1,128,768]{2,1,0:T(8,128)(2,1)}, bf16[1,128,768]{2,1,0:T(8,128)(2,1)}, bf16[1,128,768]{2,1,0:T(8,128)(2,1)}) custom-call(bf16[160,2048]{1,0:T(8,128)(2,1)} %get-tuple-element.10.refs_0_, bf16[160,2048]{1,0:T(8,128)(2,1)} %get-tuple-element.11.refs_1_, ...), custom_call_target="tpu_custom_call" | custom-call | tf_op jit(solution)/shard_map/pallas_call | solution.py:526
